TPU v7x, 256 devices: a whole 4x4x8 slice. The times are simulated.
256 devices in a mesh: src: 8 (over y, core), tgt: 32 (over x, z).
Axes of the slice: x: 4, y: 4, z: 8, core: 2. Of those that a mesh axis runs over, the one named last changes fastest.
Arguments:
- source: bfloat16 [16384, 128], P('src'), may hold values from -6 to 6
- target: bfloat16 [32768, 128], P('tgt'), may hold values from -5 to 5
- start_map: float32 [128, 128], replicated, may hold values from -1 to 1
- warm_potential: float32 [32768], P('tgt'), may hold values from -60 to 24
Outputs:
- row_potential: float32 [16384], P('src')
- col_potential: float32 [32768], P('tgt')
- new_map: float32 [128, 128], replicated
All inputs are finite; a program needn't handle non-finite values.
Results may differ from a plain program's by a relative error of at most 0.0078.
Values sent between devices are 32-bit elements; how exact they have to be, the bound alone decides.
A program may use at most 64 MiB of HBM per device.

v0:
```python
import math
import jax
import jax.numpy as jnp
from jax import lax
from jax.sharding import PartitionSpec as P

ROUNDS = 3
NEWTON = 10
EPS = 0.05


def row_partials(rotated, target, col_pot, score_scale):
    row_count = rotated.shape[0]
    block_rows = math.gcd(row_count, 512)
    blocks = rotated.reshape(row_count // block_rows, block_rows, rotated.shape[1])

    def row_one_block(row_block):
        scores = (
            jnp.einsum("rd,cd->rc", row_block, target, preferred_element_type=jnp.float32)
            * score_scale
            + col_pot[None, :]
        )
        peak_val = jnp.max(scores, axis=1)
        totals = jnp.sum(jnp.exp(scores - peak_val[:, None]), axis=1)
        return (peak_val, totals)

    peak_val, totals = lax.map(row_one_block, blocks)
    return (peak_val.reshape(row_count), totals.reshape(row_count))


def col_partials(rotated, target, row_pot, score_scale):
    row_count = rotated.shape[0]
    block_rows = math.gcd(row_count, 512)
    blocks = rotated.reshape(row_count // block_rows, block_rows, rotated.shape[1])
    pots = row_pot.reshape(row_count // block_rows, block_rows)

    def col_one_block(inputs):
        row_block, pot_block = inputs
        scores = (
            jnp.einsum("rd,cd->rc", row_block, target, preferred_element_type=jnp.float32)
            * score_scale
            + pot_block[:, None]
        )
        peak_val = jnp.max(scores, axis=0)
        totals = jnp.sum(jnp.exp(scores - peak_val[None, :]), axis=0)
        return (peak_val, totals)

    peaks, totals = lax.map(col_one_block, (blocks, pots))
    peak_val = jnp.max(peaks, axis=0)
    return (peak_val, jnp.sum(totals * jnp.exp(peaks - peak_val[None, :]), axis=0))


def across_targets(peak_val, totals):
    global_peak = lax.pmax(peak_val, "tgt")
    totals = lax.psum(totals * jnp.exp(peak_val - global_peak), "tgt")
    peak_val = global_peak
    return peak_val + jnp.log(totals)


def across_sources(peak_val, totals):
    global_peak = lax.pmax(peak_val, "src")
    totals = lax.psum(totals * jnp.exp(peak_val - global_peak), "src")
    peak_val = global_peak
    return peak_val + jnp.log(totals)


def polar(matrix):
    iterate = matrix / jnp.sqrt(jnp.sum(matrix * matrix) + 1e-06)
    for newton_index in range(NEWTON):
        gram_matrix = jnp.dot(iterate.T, iterate, precision=lax.Precision.HIGHEST)
        iterate = 1.5 * iterate - 0.5 * jnp.dot(
            iterate, gram_matrix, precision=lax.Precision.HIGHEST
        )
    return iterate


def shards(source, target, start_map, warm_potential):
    width = source.shape[1]
    score_scale = 1.0 / (math.sqrt(width) * EPS)
    rows_all = source.shape[0] * lax.axis_size("src")
    cols_all = target.shape[0] * lax.axis_size("tgt")
    rotated = jnp.dot(
        source, start_map.astype(jnp.bfloat16), preferred_element_type=jnp.float32
    ).astype(jnp.bfloat16)
    col_pot = warm_potential
    for round_index in range(ROUNDS):
        row_pot = -math.log(rows_all) - across_targets(
            *row_partials(rotated, target, col_pot, score_scale)
        )
        col_pot = -math.log(cols_all) - across_sources(
            *col_partials(rotated, target, row_pot, score_scale)
        )
    row_lse = across_targets(*row_partials(rotated, target, col_pot, score_scale))
    row_pot = -math.log(rows_all) - row_lse
    rows_here = source.shape[0] // lax.axis_size("tgt")
    block_rows = math.gcd(rows_here * lax.axis_size("tgt"), 512)
    nblocks = rows_here * lax.axis_size("tgt") // block_rows

    def numerator_one_block(inputs):
        row_block, lse_block = inputs
        scores = (
            jnp.einsum("rd,cd->rc", row_block, target, preferred_element_type=jnp.float32)
            * score_scale
            + col_pot[None, :]
            - lse_block[:, None]
        )
        weights = jnp.exp(scores).astype(jnp.bfloat16)
        return jnp.dot(weights, target, preferred_element_type=jnp.float32)

    parts_out = lax.map(
        numerator_one_block,
        (rotated.reshape(nblocks, block_rows, width), row_lse.reshape(nblocks, block_rows)),
    )
    my_targets = lax.psum_scatter(
        parts_out.reshape(rows_here * lax.axis_size("tgt"), width),
        "tgt",
        scatter_dimension=0,
        tiled=True,
    )
    source_rows = lax.dynamic_slice_in_dim(source, lax.axis_index("tgt") * rows_here, rows_here, 0)
    partial_value = jnp.einsum(
        "rd,re->de", source_rows.astype(jnp.float32), my_targets, precision=lax.Precision.HIGHEST
    )
    covariance_sum = lax.psum(partial_value, ("src", "tgt"))
    new_map = polar(covariance_sum)
    return (EPS * row_pot, EPS * col_pot, new_map)


def solution(mesh):
    placed = (P("src", None), P("tgt", None), P(), P("tgt"))
    return jax.shard_map(
        shards, mesh=mesh, in_specs=placed, out_specs=(P("src"), P("tgt"), P()), check_vma=False
    )
```

profile of v0, /device:TPU:1, one launch (start us, length us, event | category | flops | bytes accessed | tf_op | source)
XLA Modules:
  0.0 1202.2 jit_solution(3626454813866031106)
XLA Ops:
  9.4 8.7 while.94
  9.4 1.5 fusion.139
  11.6 1.5 fusion.139
  13.7 1.5 fusion.139
  15.9 1.5 fusion.139
  18.1 65.3 %pmax.49 = f32[2048]{0:T(1024)S(1)} all-reduce(f32[2048]{0:T(1024)S(1)} %bitcast.221), channel_id=1, replica_groups=mesh['src'=8,'tgt'=32] {'tgt'}, use_global_device_ids=true, to_apply=%region_4.5 | all-reduce | flops 2048 | bytes 16384 | tf_op jit(solution)/shard_map/pmax | solution.py:54
  83.4 56.8 %psum.56 = f32[2048]{0:T(1024)S(1)} all-reduce(f32[2048]{0:T(1024)S(1)} %exponential_multiply_fusion.3), channel_id=1, replica_groups=mesh['src'=8,'tgt'=32] {'tgt'}, use_global_device_ids=true, to_apply=%region_5.6 | all-reduce | flops 2048 | bytes 16384 | tf_op jit(solution)/shard_map/psum | solution.py:55
  140.3 8.4 while.95
  146.6 1.4 fusion.141
  148.7 40.6 %pmax.50 = f32[1024]{0:T(1024)S(1)} all-reduce(f32[1024]{0:T(1024)S(1)} %reduce_max.90), channel_id=1, replica_groups=mesh['src'=8,'tgt'=32] {'src'}, use_global_device_ids=true, to_apply=%region_11.12 | all-reduce | flops 1024 | bytes 8192 | tf_op jit(solution)/shard_map/pmax | solution.py:61
  189.4 12.3 %psum.57 = f32[1024]{0:T(1024)S(1)} all-reduce(f32[1024]{0:T(1024)S(1)} %exponential_multiply_fusion.6), channel_id=1, replica_groups=mesh['src'=8,'tgt'=32] {'src'}, use_global_device_ids=true, to_apply=%region_13.14 | all-reduce | flops 1024 | bytes 8192 | tf_op jit(solution)/shard_map/psum | solution.py:62
  201.7 8.7 while.96
  201.7 1.5 fusion.143
  203.9 1.5 fusion.143
  206.1 1.5 fusion.143
  208.2 1.5 fusion.143
  210.4 58.5 %pmax.51 = f32[2048]{0:T(1024)S(1)} all-reduce(f32[2048]{0:T(1024)S(1)} %bitcast.223), channel_id=1, replica_groups=mesh['src'=8,'tgt'=32] {'tgt'}, use_global_device_ids=true, to_apply=%region_18.19 | all-reduce | flops 2048 | bytes 16384 | tf_op jit(solution)/shard_map/pmax | solution.py:54
  268.9 56.8 %psum.58 = f32[2048]{0:T(1024)S(1)} all-reduce(f32[2048]{0:T(1024)S(1)} %exponential_multiply_fusion.2), channel_id=1, replica_groups=mesh['src'=8,'tgt'=32] {'tgt'}, use_global_device_ids=true, to_apply=%region_19.20 | all-reduce | flops 2048 | bytes 16384 | tf_op jit(solution)/shard_map/psum | solution.py:55
  325.8 8.4 while.97
  332.1 1.4 fusion.145
  334.2 40.5 %pmax.52 = f32[1024]{0:T(1024)S(1)} all-reduce(f32[1024]{0:T(1024)S(1)} %reduce_max.91), channel_id=1, replica_groups=mesh['src'=8,'tgt'=32] {'src'}, use_global_device_ids=true, to_apply=%region_25.26 | all-reduce | flops 1024 | bytes 8192 | tf_op jit(solution)/shard_map/pmax | solution.py:61
  374.8 12.4 %psum.59 = f32[1024]{0:T(1024)S(1)} all-reduce(f32[1024]{0:T(1024)S(1)} %exponential_multiply_fusion.5), channel_id=1, replica_groups=mesh['src'=8,'tgt'=32] {'src'}, use_global_device_ids=true, to_apply=%region_27.28 | all-reduce | flops 1024 | bytes 8192 | tf_op jit(solution)/shard_map/psum | solution.py:62
  387.2 8.7 while.98
  387.2 1.5 fusion.147
  389.4 1.5 fusion.147
  391.6 1.5 fusion.147
  393.8 1.5 fusion.147
  395.9 59.2 %pmax.53 = f32[2048]{0:T(1024)S(1)} all-reduce(f32[2048]{0:T(1024)S(1)} %bitcast.225), channel_id=1, replica_groups=mesh['src'=8,'tgt'=32] {'tgt'}, use_global_device_ids=true, to_apply=%region_32.33 | all-reduce | flops 2048 | bytes 16384 | tf_op jit(solution)/shard_map/pmax | solution.py:54
  455.1 57.0 %psum.60 = f32[2048]{0:T(1024)S(1)} all-reduce(f32[2048]{0:T(1024)S(1)} %exponential_multiply_fusion.1), channel_id=1, replica_groups=mesh['src'=8,'tgt'=32] {'tgt'}, use_global_device_ids=true, to_apply=%region_33.34 | all-reduce | flops 2048 | bytes 16384 | tf_op jit(solution)/shard_map/psum | solution.py:55
  512.2 8.4 while.99
  520.6 39.6 %pmax.54 = f32[1024]{0:T(1024)S(1)} all-reduce(f32[1024]{0:T(1024)S(1)} %reduce_max.92), channel_id=1, replica_groups=mesh['src'=8,'tgt'=32] {'src'}, use_global_device_ids=true, to_apply=%region_39.40 | all-reduce | flops 1024 | bytes 8192 | tf_op jit(solution)/shard_map/pmax | solution.py:61
  560.3 12.4 %psum.61 = f32[1024]{0:T(1024)S(1)} all-reduce(f32[1024]{0:T(1024)S(1)} %exponential_multiply_fusion.4), channel_id=1, replica_groups=mesh['src'=8,'tgt'=32] {'src'}, use_global_device_ids=true, to_apply=%region_41.42 | all-reduce | flops 1024 | bytes 8192 | tf_op jit(solution)/shard_map/psum | solution.py:62
  573.3 8.7 while.100
  573.3 1.5 fusion.151
  575.5 1.5 fusion.151
  577.7 1.5 fusion.151
  579.9 1.5 fusion.151
  582.1 59.2 %pmax.55 = f32[2048]{0:T(1024)S(1)} all-reduce(f32[2048]{0:T(1024)S(1)} %bitcast.227), channel_id=1, replica_groups=mesh['src'=8,'tgt'=32] {'tgt'}, use_global_device_ids=true, to_apply=%region_46.47 | all-reduce | flops 2048 | bytes 16384 | tf_op jit(solution)/shard_map/pmax | solution.py:54
  641.3 57.0 %psum.62 = f32[2048]{0:T(1024)S(1)} all-reduce(f32[2048]{0:T(1024)S(1)} %exponential_multiply_fusion), channel_id=1, replica_groups=mesh['src'=8,'tgt'=32] {'tgt'}, use_global_device_ids=true, to_apply=%region_47.48 | all-reduce | flops 2048 | bytes 16384 | tf_op jit(solution)/shard_map/psum | solution.py:55
  698.9 10.4 while.101
  698.9 2.6 fusion.155
  701.5 2.6 fusion.155
  704.1 2.6 fusion.155
  706.7 2.6 fusion.155
  709.6 228.3 %reduce-scatter.2.cloned.1.call-done = f32[64,128]{1,0:T(8,128)} async-done(((f32[2048,128]{1,0:T(8,128)}), f32[64,128]{1,0:T(8,128)}) %reduce-scatter.2.cloned.1.call-update) | async-done | bytes 32784 | tf_op jit(solution)/shard_map/reduce_scatter | solution.py:114
  937.9 1.6 fusion.60
  939.5 246.2 %all-reduce.2.cloned.1.call-done = f32[128,128]{1,0:T(8,128)} async-done(((f32[128,128]{1,0:T(8,128)}), f32[128,128]{1,0:T(8,128)}) %all-reduce.2.cloned.1.call-update) | async-done | bytes 65552 | tf_op jit(solution)/shard_map/psum | solution.py:124
  1185.8 1.5 multiply_reduce_fusion
  (192 shorter events, 43.9 us)
Async XLA Ops:
  7.2 1.0 copy-start
  7.2 930.7 %reduce-scatter.2.cloned.1.call-start = ((), (), s32[]{:S(2)}) async-start(), calls=%async_computation.1 | async-start | bytes 1081344 | tf_op jit(solution)/shard_map/reduce_scatter | solution.py:114
  9.4 1.5 copy-start.1
  11.6 1.5 copy-start.1
  13.7 1.5 copy-start.1
  15.9 1.5 copy-start.1
  709.4 476.4 %all-reduce.2.cloned.1.call-start = ((), (), s32[]{:S(2)}) async-start(), calls=%async_computation.2 | async-start | bytes 131072 | tf_op jit(solution)/shard_map/psum | solution.py:124
Sparse Core Ops, SparseCore 0:
  709.5 228.3 reduce-scatter.1
  944.0 241.7 all-reduce.1
where the time goes:
time: 1200 us
  blocking collectives  628 us (52%)
  waiting for transfers between devices  475 us (40%)
  matrix products  60.8 us (5%)
  other arithmetic  18 us (2%)
  between operations  15.3 us (1%)
    psum x1, waiting for transfers between devices, shards(): covariance_sum = lax.psum(partial_value, ('src', 'tgt'))  246 us
    pmax x4, blocking collectives, across_targets(): global_peak = lax.pmax(peak_val, 'tgt')  242 us
    reduce_scatter x1, waiting for transfers between devices, shards(): lax.psum_scatter(parts_out.reshape(rows_here * lax.axis_size('tgt'), widt...  228 us
    psum x4, blocking collectives, across_targets(): totals = lax.psum(totals * jnp.exp(peak_val - global_peak), 'tgt')  228 us
    pmax x3, blocking collectives, across_sources(): global_peak = lax.pmax(peak_val, 'src')  121 us
    psum x3, blocking collectives, across_sources(): totals = lax.psum(totals * jnp.exp(peak_val - global_peak), 'src')  37.1 us
  transfers between devices with their start and end apart: 2, of which 2 were waited for; matrix products, arithmetic and copies ran while one was open for 0% of the time, Pallas kernels for 0%

commit v1 on v0

--- a/solution.py
+++ b/solution.py
@@ -52,7 +52,9 @@
 
 def across_targets(peak_val, totals):
     global_peak = lax.pmax(peak_val, "tgt")
-    totals = lax.psum(totals * jnp.exp(peak_val - global_peak), "tgt")
+    x = totals * jnp.exp(peak_val - global_peak)
+    terms = lax.all_gather(x, "tgt")
+    totals = jnp.sum(terms, axis=0)
     peak_val = global_peak
     return peak_val + jnp.log(totals)
 

time: 1200 us -> 1110 us (0.925)
  blocking collectives: 628 us -> 532 us
    psum x4 -> x0, blocking collectives: 228 us -> none  [across_targets(): totals = lax.psum(totals * jnp.exp(peak_val - global_peak), 'tgt')]
    all_gather x0 -> x4, blocking collectives: none -> 137 us  [across_targets(): terms = lax.all_gather(x, 'tgt')]
where the time goes in v1:
time: 1110 us
  blocking collectives  532 us (48%)
  waiting for transfers between devices  476 us (43%)
  matrix products  60.9 us (5%)
  other arithmetic  18.2 us (2%)
  between operations  15.3 us (1%)
    psum x1, waiting for transfers between devices, shards(): covariance_sum = lax.psum(partial_value, ('src', 'tgt'))  246 us
    pmax x4, blocking collectives, across_targets(): global_peak = lax.pmax(peak_val, 'tgt')  243 us
    reduce_scatter x1, waiting for transfers between devices, shards(): lax.psum_scatter(parts_out.reshape(rows_here * lax.axis_size('tgt'), widt...  230 us
    all_gather x4, blocking collectives, across_targets(): terms = lax.all_gather(x, 'tgt')  137 us
    pmax x3, blocking collectives, across_sources(): global_peak = lax.pmax(peak_val, 'src')  115 us
    psum x3, blocking collectives, across_sources(): totals = lax.psum(totals * jnp.exp(peak_val - global_peak), 'src')  37.1 us
    dot_general x16, matrix products, row_one_block(): jnp.einsum('rd,cd->rc', row_block, target, preferred_element_type=jnp.flo...  23.6 us
  transfers between devices with their start and end apart: 2, of which 2 were waited for; matrix products, arithmetic and copies ran while one was open for 0% of the time, Pallas kernels for 0%

profile of v1, /device:TPU:1, one launch (start us, length us, event | category | flops | bytes accessed | tf_op | source)
XLA Modules:
  0.0 1107.6 jit_solution(6421580594281398857)
XLA Ops:
  9.4 8.7 while.94
  9.4 1.5 fusion.139
  11.6 1.5 fusion.139
  13.7 1.5 fusion.139
  15.9 1.5 fusion.139
  18.1 65.3 %pmax.49 = f32[2048]{0:T(1024)S(1)} all-reduce(f32[2048]{0:T(1024)S(1)} %bitcast.221), channel_id=1, replica_groups=mesh['src'=8,'tgt'=32] {'tgt'}, use_global_device_ids=true, to_apply=%region_4.5 | all-reduce | flops 2048 | bytes 16384 | tf_op jit(solution)/shard_map/pmax | solution.py:54
  83.4 34.1 %all-gather = f32[65536]{0:T(1024)S(1)} all-gather(f32[2048]{0:T(1024)S(1)} %exponential_multiply_fusion.3), channel_id=2, replica_groups=mesh['src'=8,'tgt'=32] {'tgt'}, dimensions={0}, use_global_device_ids=true | all-gather | bytes 270336 | tf_op jit(solution)/shard_map/all_gather | solution.py:56
  117.7 8.4 while.95
  121.9 1.4 fusion.141
  126.1 38.5 %pmax.50 = f32[1024]{0:T(1024)S(1)} all-reduce(f32[1024]{0:T(1024)S(1)} %reduce_max.90), channel_id=1, replica_groups=mesh['src'=8,'tgt'=32] {'src'}, use_global_device_ids=true, to_apply=%region_11.12 | all-reduce | flops 1024 | bytes 8192 | tf_op jit(solution)/shard_map/pmax | solution.py:63
  164.7 12.3 %psum.28 = f32[1024]{0:T(1024)S(1)} all-reduce(f32[1024]{0:T(1024)S(1)} %exponential_multiply_fusion.6), channel_id=1, replica_groups=mesh['src'=8,'tgt'=32] {'src'}, use_global_device_ids=true, to_apply=%region_13.14 | all-reduce | flops 1024 | bytes 8192 | tf_op jit(solution)/shard_map/psum | solution.py:64
  177.0 8.7 while.96
  177.0 1.5 fusion.143
  179.2 1.5 fusion.143
  181.4 1.5 fusion.143
  183.5 1.5 fusion.143
  185.7 59.1 %pmax.51 = f32[2048]{0:T(1024)S(1)} all-reduce(f32[2048]{0:T(1024)S(1)} %bitcast.223), channel_id=1, replica_groups=mesh['src'=8,'tgt'=32] {'tgt'}, use_global_device_ids=true, to_apply=%region_18.19 | all-reduce | flops 2048 | bytes 16384 | tf_op jit(solution)/shard_map/pmax | solution.py:54
  244.9 34.2 %all-gather.1 = f32[65536]{0:T(1024)S(1)} all-gather(f32[2048]{0:T(1024)S(1)} %exponential_multiply_fusion.2), channel_id=3, replica_groups=mesh['src'=8,'tgt'=32] {'tgt'}, dimensions={0}, use_global_device_ids=true | all-gather | bytes 270336 | tf_op jit(solution)/shard_map/all_gather | solution.py:56
  279.2 8.4 while.97
  283.4 1.4 fusion.145
  287.6 38.4 %pmax.52 = f32[1024]{0:T(1024)S(1)} all-reduce(f32[1024]{0:T(1024)S(1)} %reduce_max.91), channel_id=1, replica_groups=mesh['src'=8,'tgt'=32] {'src'}, use_global_device_ids=true, to_apply=%region_25.26 | all-reduce | flops 1024 | bytes 8192 | tf_op jit(solution)/shard_map/pmax | solution.py:63
  326.0 12.4 %psum.29 = f32[1024]{0:T(1024)S(1)} all-reduce(f32[1024]{0:T(1024)S(1)} %exponential_multiply_fusion.5), channel_id=1, replica_groups=mesh['src'=8,'tgt'=32] {'src'}, use_global_device_ids=true, to_apply=%region_27.28 | all-reduce | flops 1024 | bytes 8192 | tf_op jit(solution)/shard_map/psum | solution.py:64
  338.4 8.7 while.98
  338.5 1.5 fusion.147
  340.6 1.5 fusion.147
  342.8 1.5 fusion.147
  345.0 1.5 fusion.147
  347.2 59.1 %pmax.53 = f32[2048]{0:T(1024)S(1)} all-reduce(f32[2048]{0:T(1024)S(1)} %bitcast.225), channel_id=1, replica_groups=mesh['src'=8,'tgt'=32] {'tgt'}, use_global_device_ids=true, to_apply=%region_32.33 | all-reduce | flops 2048 | bytes 16384 | tf_op jit(solution)/shard_map/pmax | solution.py:54
  406.3 34.1 %all-gather.2 = f32[65536]{0:T(1024)S(1)} all-gather(f32[2048]{0:T(1024)S(1)} %exponential_multiply_fusion.1), channel_id=4, replica_groups=mesh['src'=8,'tgt'=32] {'tgt'}, dimensions={0}, use_global_device_ids=true | all-gather | bytes 270336 | tf_op jit(solution)/shard_map/all_gather | solution.py:56
  440.6 8.4 while.99
  449.0 38.4 %pmax.54 = f32[1024]{0:T(1024)S(1)} all-reduce(f32[1024]{0:T(1024)S(1)} %reduce_max.92), channel_id=1, replica_groups=mesh['src'=8,'tgt'=32] {'src'}, use_global_device_ids=true, to_apply=%region_39.40 | all-reduce | flops 1024 | bytes 8192 | tf_op jit(solution)/shard_map/pmax | solution.py:63
  487.4 12.4 %psum.30 = f32[1024]{0:T(1024)S(1)} all-reduce(f32[1024]{0:T(1024)S(1)} %exponential_multiply_fusion.4), channel_id=1, replica_groups=mesh['src'=8,'tgt'=32] {'src'}, use_global_device_ids=true, to_apply=%region_41.42 | all-reduce | flops 1024 | bytes 8192 | tf_op jit(solution)/shard_map/psum | solution.py:64
  500.4 8.7 while.100
  500.4 1.5 fusion.151
  502.6 1.5 fusion.151
  504.8 1.5 fusion.151
  507.0 1.5 fusion.151
  509.2 59.1 %pmax.55 = f32[2048]{0:T(1024)S(1)} all-reduce(f32[2048]{0:T(1024)S(1)} %bitcast.227), channel_id=1, replica_groups=mesh['src'=8,'tgt'=32] {'tgt'}, use_global_device_ids=true, to_apply=%region_46.47 | all-reduce | flops 2048 | bytes 16384 | tf_op jit(solution)/shard_map/pmax | solution.py:54
  568.3 34.3 %all-gather.3 = f32[65536]{0:T(1024)S(1)} all-gather(f32[2048]{0:T(1024)S(1)} %exponential_multiply_fusion), channel_id=5, replica_groups=mesh['src'=8,'tgt'=32] {'tgt'}, dimensions={0}, use_global_device_ids=true | all-gather | bytes 270336 | tf_op jit(solution)/shard_map/all_gather | solution.py:56
  603.3 10.4 while.101
  603.3 2.6 fusion.155
  605.9 2.6 fusion.155
  608.5 2.6 fusion.155
  611.1 2.6 fusion.155
  613.8 229.7 %reduce-scatter.2.cloned.1.call-done = f32[64,128]{1,0:T(8,128)} async-done(((f32[2048,128]{1,0:T(8,128)}), f32[64,128]{1,0:T(8,128)}) %reduce-scatter.2.cloned.1.call-update) | async-done | bytes 32784 | tf_op jit(solution)/shard_map/reduce_scatter | solution.py:116
  843.5 1.6 fusion.60
  845.1 246.0 %all-reduce.2.cloned.1.call-done = f32[128,128]{1,0:T(8,128)} async-done(((f32[128,128]{1,0:T(8,128)}), f32[128,128]{1,0:T(8,128)}) %all-reduce.2.cloned.1.call-update) | async-done | bytes 65552 | tf_op jit(solution)/shard_map/psum | solution.py:126
  1091.1 1.5 multiply_reduce_fusion
  (200 shorter events, 44.0 us)
Async XLA Ops:
  7.2 1.0 copy-start
  7.2 836.3 %reduce-scatter.2.cloned.1.call-start = ((), (), s32[]{:S(2)}) async-start(), calls=%async_computation.1 | async-start | bytes 1081344 | tf_op jit(solution)/shard_map/reduce_scatter | solution.py:116
  9.4 1.5 copy-start.1
  11.6 1.5 copy-start.1
  13.7 1.5 copy-start.1
  15.9 1.5 copy-start.1
  613.7 477.4 %all-reduce.2.cloned.1.call-start = ((), (), s32[]{:S(2)}) async-start(), calls=%async_computation.2 | async-start | bytes 131072 | tf_op jit(solution)/shard_map/psum | solution.py:126
Sparse Core Ops, SparseCore 0:
  613.9 229.5 reduce-scatter.1
  849.6 241.4 all-reduce.1
